TPU v7x, 256 devices: a whole 4x4x8 slice. The times are simulated.
256 devices in a mesh: dp: 2 (over x_lo), row: 8 (over y, core), col: 16 (over z, x_hi).
Axes of the slice: x: 4 (x_hi: 2, x_lo: 2; x = x_hi * 2 + x_lo), y: 4, z: 8, core: 2. Of those that a mesh axis runs over, the one named last changes fastest.
Arguments:
- inputs: bfloat16 [1280, 12288], P(('dp', 'row'), 'col'), may hold values from -3 to 3
- upstream: bfloat16 [1280, 12288], P(('dp', 'row'), 'col'), may hold values from -3 to 3
- preact: bfloat16 [1280, 2, 12288], P(('dp', 'col'), None, 'row'), may hold values from -5 to 5
- w_in: bfloat16 [12288, 2, 12288], P('col', 'dp', 'row'), may hold values from -0.0546875 to 0.0546875
- w_out: bfloat16 [2, 12288, 12288], P('dp', 'row', 'col'), may hold values from -0.0390625 to 0.0390625
Outputs:
- grad_in: bfloat16 [1280, 12288], P(('dp', 'row'), 'col')
- grad_w_in: bfloat16 [12288, 2, 12288], P('col', 'dp', 'row')
- grad_w_out: bfloat16 [2, 12288, 12288], P('dp', 'row', 'col')
All inputs are finite; a program needn't handle non-finite values.
Results may differ from a plain program's by a relative error of at most 0.006.
Values may be sent and summed in bfloat16 or wider, within the bound.
A program may use at most 128 MiB of HBM per device.

v0:
```python
import jax
import jax.numpy as jnp
from jax import lax
from jax.sharding import PartitionSpec as P

GELU_C = 0.7978845608028654
GELU_K = 0.044715


def gelu_parts(values):
    wide = values.astype(jnp.float32)
    inner = jnp.tanh(GELU_C * (wide + GELU_K * wide * wide * wide))
    active = 0.5 * wide * (1.0 + inner)
    slope = 0.5 * (1.0 + inner) + 0.5 * wide * (1.0 - inner * inner) * GELU_C * (
        1.0 + 3.0 * GELU_K * wide * wide
    )
    return (active, slope)


def right_product(source, matrix):
    return lax.dot_general(
        source, matrix, (((1,), (1,)), ((), ())), preferred_element_type=jnp.float32
    )


def body(inputs, upstream, preact, w_in, w_out):
    d_cols = inputs.shape[1]
    n_dp = lax.axis_size("dp")
    w_in_full, w_out_full = (
        lax.all_gather(w_in, "dp", axis=1, tiled=True),
        lax.all_gather(w_out, "dp", axis=0, tiled=True),
    )
    inputs_all, upstream_all = (
        lax.all_gather(inputs, "row", axis=0, tiled=True),
        lax.all_gather(upstream, "row", axis=0, tiled=True),
    )
    units = w_out_full.shape[0] * w_out_full.shape[1]
    w_out_mat = w_out_full.reshape(units, d_cols)
    w_in_mat = w_in_full.reshape(d_cols, units)
    back = lax.psum_scatter(
        right_product(upstream_all, w_out_mat), "col", scatter_dimension=0, tiled=True
    )
    pre_own = preact.reshape(preact.shape[0], units)
    active, slope = gelu_parts(pre_own)
    grad_pre = (back * slope).astype(jnp.bfloat16)
    act_low = active.astype(jnp.bfloat16)
    grad_all, act_all = (
        lax.all_gather(grad_pre, "col", axis=0, tiled=True),
        lax.all_gather(act_low, "col", axis=0, tiled=True),
    )
    grad_in = lax.psum_scatter(
        right_product(grad_all, w_in_mat), "row", scatter_dimension=0, tiled=True
    ).astype(jnp.bfloat16)
    part_in = lax.dot_general(
        inputs_all, grad_all, (((0,), (0,)), ((), ())), preferred_element_type=jnp.float32
    )
    part_out = lax.dot_general(
        act_all, upstream_all, (((0,), (0,)), ((), ())), preferred_element_type=jnp.float32
    )
    summed_in, summed_out = (
        lax.psum_scatter(
            part_in.reshape(d_cols, n_dp, units // n_dp).astype(jnp.bfloat16),
            "dp",
            scatter_dimension=1,
            tiled=True,
        ).astype(jnp.float32),
        lax.psum_scatter(
            part_out.reshape(n_dp, units // n_dp, d_cols).astype(jnp.bfloat16),
            "dp",
            scatter_dimension=0,
            tiled=True,
        ).astype(jnp.float32),
    )
    grad_w_in = summed_in.astype(jnp.bfloat16)
    grad_w_out = summed_out.astype(jnp.bfloat16)
    return (grad_in, grad_w_in, grad_w_out)


def solution(mesh):
    return jax.shard_map(
        body,
        mesh=mesh,
        in_specs=(
            P(("dp", "row"), "col"),
            P(("dp", "row"), "col"),
            P(("dp", "col"), None, "row"),
            P("col", "dp", "row"),
            P("dp", "row", "col"),
        ),
        out_specs=(P(("dp", "row"), "col"), P("col", "dp", "row"), P("dp", "row", "col")),
        check_vma=False,
    )
```

profile of v0, /device:TPU:16, one launch (start us, length us, event | category | flops | bytes accessed | tf_op | source)
XLA Modules:
  0.0 760.3 jit_solution(6873413106186094135)
XLA Ops:
  7.2 0.0 all-gather.5.cloned.1.call-start
  7.2 0.7 all-gather.5.cloned.1.call-update
  7.9 0.0 reduce-scatter.5.cloned.1.call-start
  7.9 13.9 %all_gather.18 = bf16[640,768]{1,0:T(8,128)(2,1)S(1)} all-gather(bf16[80,768]{1,0:T(8,128)(2,1)} %param.6), channel_id=1, replica_groups=mesh['dp'=2,'row'=8,'col'=16] {'row'}, dimensions={0}, use_global_device_ids=true | all-gather | bytes 1105920 | tf_op jit(solution)/shard_map/all_gather | solution.py:35
  21.9 58.4 %all-gather.5.cloned.1.call-done = bf16[2,1536,768]{2,1,0:T(8,128)(2,1)} async-done(((bf16[1,1536,768]{2,1,0:T(8,128)(2,1)}), bf16[2,1536,768]{2,1,0:T(8,128)(2,1)}) %all-gather.5.cloned.1.call-update) | async-done | bytes 4718608 | tf_op jit(solution)/shard_map/all_gather | solution.py:31
  80.3 7.7 %fusion.7 = f32[640,3072]{1,0:T(8,128)} fusion(bf16[640,768]{1,0:T(8,128)(2,1)S(1)} %all_gather.18, bf16[3072,768]{1,0:T(8,128)(2,1)} %bitcast.22), kind=kOutput, calls=%fused_computation.12 | convolution fusion | flops 3019898880 | bytes 13565952 | tf_op jit(solution)/shard_map/dot_general | solution.py:21
  88.0 0.0 copy-start
  88.0 0.0 reduce-scatter.5.cloned.1.call-update
  88.0 0.0 all-gather.9.cloned.1.call-start
  88.1 0.7 all-gather.9.cloned.1.call-update
  88.8 0.0 all-gather.7.cloned.1.call-start
  88.8 0.1 copy-done
  89.0 225.3 %reduce-scatter.5.cloned.1.call-done = f32[40,3072]{1,0:T(8,128)} async-done(((f32[640,3072]{1,0:T(8,128)}), f32[40,3072]{1,0:T(8,128)}) %reduce-scatter.5.cloned.1.call-update) | async-done | bytes 491536 | tf_op jit(solution)/shard_map/reduce_scatter | solution.py:40
  314.3 2.1 multiply_convert_fusion
  316.4 0.0 all-gather.7.cloned.1.call-update
  316.4 0.0 all-gather.11.cloned.1.call-start
  316.5 0.5 all-gather.11.cloned.1.call-update
  317.0 0.0 reduce-scatter.7.cloned.1.call-start
  317.1 64.7 %all-gather.9.cloned.1.call-done = bf16[768,2,1536]{2,0,1:T(8,128)(2,1)} async-done(((bf16[768,1,1536]{2,0,1:T(8,128)(2,1)}), bf16[768,2,1536]{2,0,1:T(8,128)(2,1)}) %all-gather.9.cloned.1.call-update) | async-done | bytes 4718608 | tf_op jit(solution)/shard_map/all_gather | solution.py:30
  381.8 6.6 copy.11
  388.4 95.8 %all-gather.7.cloned.1.call-done = bf16[640,3072]{1,0:T(8,128)(2,1)} async-done(((bf16[40,3072]{1,0:T(8,128)(2,1)}), bf16[640,3072]{1,0:T(8,128)(2,1)}) %all-gather.7.cloned.1.call-update) | async-done | bytes 3932176 | tf_op jit(solution)/shard_map/all_gather | solution.py:48
  484.2 0.0 copy-start.1
  484.2 8.1 %fusion.8 = f32[640,768]{1,0:T(8,128)} fusion(bf16[640,3072]{1,0:T(8,128)(2,1)} %all-gather.7.cloned.1.call-done, bf16[768,3072]{0,1:T(8,128)(2,1)} %bitcast.18), kind=kOutput, calls=%fused_computation.13 | convolution fusion | flops 3019898880 | bytes 10616832 | tf_op jit(solution)/shard_map/dot_general | solution.py:21
  492.3 0.0 reduce-scatter.7.cloned.1.call-update
  492.3 0.0 reduce-scatter.9.cloned.1.call-start
  492.3 0.0 copy-done.1
  492.3 12.5 %all_gather.22 = bf16[640,768]{1,0:T(8,128)(2,1)S(1)} all-gather(bf16[80,768]{1,0:T(8,128)(2,1)S(1)} %copy-done.1), channel_id=1, replica_groups=mesh['dp'=2,'row'=8,'col'=16] {'row'}, dimensions={0}, use_global_device_ids=true | all-gather | bytes 1105920 | tf_op jit(solution)/shard_map/all_gather | solution.py:34
  504.9 7.7 %convolution_convert_fusion.1 = bf16[3072,768]{1,0:T(8,128)(2,1)} fusion(bf16[640,3072]{1,0:T(8,128)(2,1)} %all-gather.7.cloned.1.call-done, bf16[640,768]{1,0:T(8,128)(2,1)S(1)} %all_gather.22), kind=kOutput, calls=%fused_computation.1 | convolution fusion | flops 3022258176 | bytes 9633792 | tf_op jit(solution)/shard_map/dot_general | solution.py:54
  512.6 6.7 copy.12
  519.3 0.0 reduce-scatter.9.cloned.1.call-update
  519.3 0.0 reduce-scatter.11.cloned.1.call-start
  519.4 62.7 %all-gather.11.cloned.1.call-done = bf16[640,3072]{1,0:T(8,128)(2,1)} async-done(((bf16[40,3072]{1,0:T(8,128)(2,1)}), bf16[640,3072]{1,0:T(8,128)(2,1)}) %all-gather.11.cloned.1.call-update) | async-done | bytes 3932176 | tf_op jit(solution)/shard_map/all_gather | solution.py:49
  582.1 7.7 %convolution_convert_fusion = bf16[3072,768]{1,0:T(8,128)(2,1)} fusion(bf16[640,3072]{1,0:T(8,128)(2,1)} %all-gather.11.cloned.1.call-done, bf16[640,768]{1,0:T(8,128)(2,1)S(1)} %all_gather.18), kind=kOutput, calls=%fused_computation | convolution fusion | flops 3022258176 | bytes 9633792 | tf_op jit(solution)/shard_map/dot_general | solution.py:57
  589.8 0.0 reduce-scatter.11.cloned.1.call-update
  589.8 22.2 %reduce-scatter.7.cloned.1.call-done = f32[80,768]{1,0:T(8,128)} async-done(((f32[640,768]{1,0:T(8,128)}), f32[80,768]{1,0:T(8,128)}) %reduce-scatter.7.cloned.1.call-update) | async-done | bytes 245776 | tf_op jit(solution)/shard_map/reduce_scatter | solution.py:51
  612.0 1.6 convert_element_type.37
  613.7 70.6 %reduce-scatter.9.cloned.1.call-done = bf16[768,1,1536]{2,0,1:T(8,128)(2,1)} async-done(((bf16[768,2,1536]{2,0,1:T(8,128)(2,1)}), bf16[768,1,1536]{2,0,1:T(8,128)(2,1)}) %reduce-scatter.9.cloned.1.call-update) | async-done | bytes 2359312 | tf_op jit(solution)/shard_map/reduce_scatter | solution.py:61
  684.2 69.2 %reduce-scatter.11.cloned.1.call-done = bf16[1,1536,768]{2,1,0:T(8,128)(2,1)} async-done(((bf16[2,1536,768]{2,1,0:T(8,128)(2,1)}), bf16[1,1536,768]{2,1,0:T(8,128)(2,1)}) %reduce-scatter.11.cloned.1.call-update) | async-done | bytes 2359312 | tf_op jit(solution)/shard_map/reduce_scatter | solution.py:67
  (1 shorter events, 0.0 us)
Async XLA Ops:
  7.2 73.2 %all-gather.5.cloned.1.call-start = ((), (), s32[]{:S(2)}) async-start(), calls=%async_computation.4 | async-start | bytes 7077888 | tf_op jit(solution)/shard_map/all_gather | solution.py:31
  7.9 306.4 %reduce-scatter.5.cloned.1.call-start = ((), (), s32[]{:S(2)}) async-start(), calls=%async_computation.5 | async-start | bytes 8355840 | tf_op jit(solution)/shard_map/reduce_scatter | solution.py:40
  88.0 0.9 copy-start
  88.0 293.8 %all-gather.9.cloned.1.call-start = ((), (), s32[]{:S(2)}) async-start(), calls=%async_computation.7 | async-start | bytes 7077888 | tf_op jit(solution)/shard_map/all_gather | solution.py:30
  88.8 395.4 %all-gather.7.cloned.1.call-start = ((), (), s32[]{:S(2)}) async-start(), calls=%async_computation.6 | async-start | bytes 4177920 | tf_op jit(solution)/shard_map/all_gather | solution.py:48
  316.4 265.7 %all-gather.11.cloned.1.call-start = ((), (), s32[]{:S(2)}) async-start(), calls=%async_computation.10 | async-start | bytes 4177920 | tf_op jit(solution)/shard_map/all_gather | solution.py:49
  317.0 295.0 %reduce-scatter.7.cloned.1.call-start = ((), (), s32[]{:S(2)}) async-start(), calls=%async_computation.8 | async-start | bytes 2211840 | tf_op jit(solution)/shard_map/reduce_scatter | solution.py:51
  484.2 8.1 %copy-start.1 = (bf16[80,768]{1,0:T(8,128)(2,1)S(1)}, bf16[80,768]{1,0:T(8,128)(2,1)}, u32[]{:S(2)}) copy-start(bf16[80,768]{1,0:T(8,128)(2,1)} %param.5) | copy-start | bytes 368644
  492.3 192.0 %reduce-scatter.9.cloned.1.call-start = ((), (), s32[]{:S(2)}) async-start(), calls=%async_computation.9 | async-start | bytes 7077888 | tf_op jit(solution)/shard_map/reduce_scatter | solution.py:61
  519.3 234.2 %reduce-scatter.11.cloned.1.call-start = ((), (), s32[]{:S(2)}) async-start(), calls=%async_computation.11 | async-start | bytes 7077888 | tf_op jit(solution)/shard_map/reduce_scatter | solution.py:67
Sparse Core Ops, SparseCore 0:
  9.8 70.5 all-gather.4
  88.1 226.0 reduce-scatter.4
  316.1 65.6 all-gather.8
  384.8 99.3 all-gather.6
  487.2 94.8 all-gather.10
  584.5 27.4 reduce-scatter.6
  615.3 68.8 reduce-scatter.8
  687.4 66.0 reduce-scatter.10
where the time goes:
time: 762 us; the launch traced here: 760 us
  waiting for transfers between devices  671 us (88%)
  matrix products  31.2 us (4%)
  blocking collectives  26.5 us (3%)
  between operations  14.2 us (2%)
  local copies, waits for them, and re-layouts  13.5 us (2%)
    reduce_scatter x1, waiting for transfers between devices, body(): lax.psum_scatter(right_product(upstream_all, w_out_mat), 'col', scatter_d...  225 us
    all_gather x1, waiting for transfers between devices, body(): lax.all_gather(grad_pre, 'col', axis=0, tiled=True)  95.8 us
    reduce_scatter x1, waiting for transfers between devices, body(): lax.psum_scatter(part_in.reshape(d_cols, n_dp, units // n_dp).astype(jnp....  70.6 us
    reduce_scatter x1, waiting for transfers between devices, body(): lax.psum_scatter(part_out.reshape(n_dp, units // n_dp, d_cols).astype(jnp...  69.2 us
    all_gather x1, waiting for transfers between devices, body(): lax.all_gather(w_in, 'dp', axis=1, tiled=True)  64.7 us
    all_gather x1, waiting for transfers between devices, body(): lax.all_gather(act_low, 'col', axis=0, tiled=True)  62.7 us
    all_gather x1, waiting for transfers between devices, body(): lax.all_gather(w_out, 'dp', axis=0, tiled=True)  58.4 us
    reduce_scatter x1, waiting for transfers between devices, body(): lax.psum_scatter(right_product(grad_all, w_in_mat), 'row', scatter_dimens...  22.2 us
  transfers between devices with their start and end apart: 8, of which 8 were waited for; matrix products, arithmetic and copies ran while one was open for 5% of the time, Pallas kernels for 0%

commit v1 on v0

v1 whole, which is shorter than its diff:
```python
import functools

import jax
import jax.numpy as jnp
from jax import lax
from jax.experimental import pallas as pl
from jax.experimental.pallas import tpu as pltpu
from jax.sharding import PartitionSpec as P

GELU_C = 0.7978845608028654
GELU_K = 0.044715
MESH = pl.DeviceIdType.MESH
BF = jnp.bfloat16
F32 = jnp.float32

B = 80
D = 768
H = 1536
HA = 768
HB = H - HA
HD = D // 2
SIGN = (1, -1)


def gelu_parts(wide):
    inner = jnp.tanh(GELU_C * (wide + GELU_K * wide * wide * wide))
    active = 0.5 * wide * (1.0 + inner)
    slope = 0.5 * (1.0 + inner) + 0.5 * wide * (1.0 - inner * inner) * GELU_C * (
        1.0 + 3.0 * GELU_K * wide * wide
    )
    return active, slope


def dot(a, b, ca, cb):
    return lax.dot_general(a, b, (((ca,), (cb,)), ((), ())), preferred_element_type=F32)


def cols_of(lane):
    return pl.ds(0, HA) if lane < 2 else pl.ds(HA, HB)


def half_of(lane, part):
    if lane < 2:
        return pl.ds(part * (HA // 2), HA // 2)
    return pl.ds(HA + part * (HB // 2), HB // 2)


def kernel(
    inp, ups, pre, w_in, w_out,
    gin_o, gwin_o, gwout_o,
    UI, AG, PB, WI, WO, PRE, SL, RA, SA, RB, SB, XBr, XBs, XA, CS, Q, GO, GI, PO, PI,
    w_sem, o_sem, p_r, p_s, u_r, u_s, u_f, z_r, z_s, xa_r, xa_s, xb_r, xb_s,
    rz_r, rz_s, rxb_r, rxb_s, rxa, cs_r, cs_s, gi_r, gi_s,
):
    dp, row, col = lax.axis_index("dp"), lax.axis_index("row"), lax.axis_index("col")
    y, core = lax.div(row, 2), lax.rem(row, 2)
    z, xh = lax.div(col, 2), lax.rem(col, 2)
    xo = 1 - xh
    me_d = dp * 8 + row
    chip_d = dp * 4 + y
    n_me = xh * 8 + z

    def zrel(d):
        return lax.rem(z + (d + 8), 8)

    def blk(lane, d):
        return (xo if lane == 1 else xh) * 8 + zrel(d)

    nbr = tuple((dp, row, zrel(s) * 2 + xh) for s in SIGN)
    partner = (dp, row, z * 2 + xo)
    sib = (dp, y * 2 + (1 - core), col)

    def rc(src, dst, ss, rs, dev):
        return pltpu.make_async_remote_copy(
            src_ref=src, dst_ref=dst, send_sem=ss, recv_sem=rs, device_id=dev, device_id_type=MESH
        )

    def got(ref, sem):
        pltpu.make_async_copy(ref, ref, sem).wait()

    wcopy_out = pltpu.make_async_copy(w_out, WO, w_sem.at[0])
    wcopy_in = pltpu.make_async_copy(w_in, WI, w_sem.at[1])
    wcopy_out.start()
    wcopy_in.start()

    barrier = pltpu.get_barrier_semaphore()

    def greet(dev):
        pl.semaphore_signal(barrier, inc=1, device_id=dev, device_id_type=MESH)

    def greet_group(j, _):
        t = lax.rem(me_d + j, 16)
        greet((lax.div(t, 8), lax.rem(t, 8), col))
        return 0

    lax.fori_loop(1, 16, greet_group, 0)
    greet(nbr[0])
    greet(nbr[1])
    greet(partner)
    greet((1 - dp, row, z * 2 + xo))
    UI[0, me_d] = ups[...]
    UI[1, me_d] = inp[...]
    pl.semaphore_wait(barrier, 19)

    def feature_start(a):
        own = UI.at[a, me_d]

        def send(j, _):
            t = lax.rem(chip_d + j, 8)
            dev = (lax.div(t, 4), lax.rem(t, 4) * 2 + core, col)
            rc(own, own, u_s.at[a, j], u_r.at[a, me_d], dev).start()
            return 0

        lax.fori_loop(1, 8, send, 0)
        rc(own, own, u_f.at[a, 0], u_r.at[a, me_d], sib).start()

    def feature_pass(a):
        def step(j, _):
            t = lax.rem(chip_d + 8 - j, 8)
            n = lax.div(t, 4) * 8 + lax.rem(t, 4) * 2 + core
            ref = UI.at[a, n]
            got(ref, u_r.at[a, n])
            rc(ref, ref, u_f.at[a, j], u_r.at[a, n], sib).start()
            return 0

        lax.fori_loop(1, 8, step, 0)

    def feature_end(a):
        def step(j, _):
            n = j * 2 + (1 - core)
            got(UI.at[a, n], u_r.at[a, n])
            return 0

        lax.fori_loop(0, 8, step, 0)

    feature_start(0)

    for k in range(2):
        own = jnp.logical_and(dp == k, dp == xh)
        src, dst = pre.at[k], PRE.at[xh]

        @pl.when(own)
        def _():
            pltpu.make_async_copy(src, dst, p_r.at[xh]).start()

        @pl.when(jnp.logical_not(own))
        def _():
            rc(src, dst, p_s.at[k], p_r.at[xh], (k, row, z * 2 + dp)).start()

    feature_start(1)

    got(PRE.at[0], p_r.at[0])
    got(PRE.at[1], p_r.at[1])
    wide = jnp.concatenate([PRE[0].astype(F32)[:40], PRE[1].astype(F32)[:40]], axis=0)
    active, slope = gelu_parts(wide)
    AG[0, n_me] = active.astype(BF)
    SL[...] = slope

    def z_send(a, di, h, lane, d):
        cols = cols_of(lane) if h < 4 else half_of(lane, di)
        ref = AG.at[a, blk(lane, d), :, cols]
        rc(ref, ref, z_s.at[a, di, h - 1, lane], z_r.at[a, di, h - 1, lane], nbr[di]).start()

    def z_got(a, di, h, lane, d):
        cols = cols_of(lane) if h < 4 else half_of(lane, di)
        got(AG.at[a, blk(lane, d), :, cols], z_r.at[a, di, h - 1, lane])

    def xb_send(a, d):
        ref = AG.at[a, blk(2, d), :, cols_of(2)]
        rc(ref, ref, xb_s.at[a, d % 8], xb_r.at[a, d % 8], partner).start()

    def xb_got(a, d):
        got(AG.at[a, blk(1, d), :, cols_of(2)], xb_r.at[a, d % 8])

    def ag_start(a):
        ref = AG.at[a, n_me, :, cols_of(0)]
        rc(ref, ref, xa_s.at[a], xa_r.at[a], partner).start()
        for lane in (0, 2):
            for di in range(2):
                z_send(a, di, 1, lane, 0)
        xb_send(a, 0)

    def ag_pair(a):
        got(AG.at[a, xo * 8 + z, :, cols_of(1)], xa_r.at[a])
        for di in range(2):
            z_send(a, di, 1, 1, 0)

    def ag_step(a, h):
        for lane in (0, 2, 1):
            for di, s in enumerate(SIGN):
                z_got(a, di, h, lane, -s * h)
                z_send(a, di, h + 1, lane, -s * h)
                if lane == 2:
                    xb_send(a, -s * h)

    def ag_last(a):
        for lane in (2, 0, 1):
            for di, s in enumerate(SIGN):
                z_got(a, di, 4, lane, -s * 4)
            if lane == 2:
                xb_send(a, 4)

    def ag_drain(a):
        rc(AG.at[a, 0, :, cols_of(0)], AG.at[a, 0, :, cols_of(0)], xa_s.at[a], xa_r.at[a], partner).wait_send()
        for d in range(8):
            ref = AG.at[a, 0, :, cols_of(2)]
            rc(ref, ref, xb_s.at[a, d], xb_r.at[a, d], partner).wait_send()
        for h in range(1, 5):
            for lane in range(3):
                for di in range(2):
                    ref = AG.at[a, 0, :, cols_of(lane) if h < 4 else half_of(lane, di)]
                    rc(ref, ref, z_s.at[a, di, h - 1, lane], z_r.at[a, di, h - 1, lane], nbr[di]).wait_send()

    ag_start(0)
    feature_pass(0)
    ag_pair(0)
    feature_end(0)
    ag_step(0, 1)

    wcopy_out.wait()

    def back_tile(i, _):
        m, t = lax.div(i, 6), lax.rem(i, 6)
        left = UI[0, pl.ds(m * 8, 8)].reshape(8 * B, D)
        rows = pl.ds(pl.multiple_of(t * 256, 256), 256)
        PB[pl.ds(m * 8, 8), :, rows] = dot(left, WO[rows, :], 1, 1).reshape(8, B, 256)
        return 0

    lax.fori_loop(0, 12, back_tile, 0)
    ag_step(0, 2)

    def rs_refs(di, s, lane):
        if lane < 2:
            cols = slice(None) if s else pl.ds(di * (HA // 2), HA // 2)
            return SA.at[di, s, lane, :, cols], RA.at[di, s, lane, :, cols]
        cols = slice(None) if s else pl.ds(di * (HB // 2), HB // 2)
        return SB.at[di, s, :, cols], RB.at[di, s, :, cols]

    def rs_send(di, s, lane):
        src, dst = rs_refs(di, s, lane)
        rc(src, dst, rz_s.at[di, s, lane], rz_r.at[di, s, lane], nbr[di]).start()

    def rs_got(di, s, lane):
        dst = rs_refs(di, s, lane)[1]
        got(dst, rz_r.at[di, s, lane])
        return dst[...].astype(F32)

    def part_of(lane, d):
        if lane < 2:
            return PB[blk(lane, d), :, cols_of(lane)]
        got(XBr.at[d % 8], rxb_r.at[d % 8])
        return PB[blk(lane, d), :, cols_of(2)] + XBr[d % 8].astype(F32)

    def rs_start_x():
        for d in (4, 3, 5, 2, 6, 1, 7, 0):
            XBs[d] = PB[blk(1, d), :, cols_of(2)].astype(BF)
            rc(XBs.at[d], XBr.at[d], rxb_s.at[d], rxb_r.at[d], partner).start()

    def rs_start_z(lane):
        val = part_of(lane, 4)
        for di in range(2):
            src = rs_refs(di, 0, lane)[0]
            width = (HA if lane < 2 else HB) // 2
            src[...] = val[:, di * width:(di + 1) * width].astype(BF)
            rs_send(di, 0, lane)

    def rs_step(s):
        for lane in range(3):
            for di, sg in enumerate(SIGN):
                come = rs_got(di, s, lane)
                val = part_of(lane, sg * (3 - s))
                full = rs_refs(di, s + 1, lane)[0]
                if s == 0:
                    width = val.shape[1] // 2
                    halves = [val[:, :width], val[:, width:]]
                    halves[di] = halves[di] + come
                    val = jnp.concatenate(halves, axis=1)
                else:
                    val = val + come
                full[...] = val.astype(BF)
                rs_send(di, s + 1, lane)

    def rs_last():
        other = part_of(1, 0) + rs_got(0, 3, 1) + rs_got(1, 3, 1)
        XA[0] = other.astype(BF)
        rc(XA.at[0], XA.at[1], rxa.at[0], rxa.at[1], partner).start()
        total = part_of(2, 0) + rs_got(0, 3, 2) + rs_got(1, 3, 2)
        AG[1, n_me, :, cols_of(2)] = (total * SL[:, cols_of(2)]).astype(BF)
        total = part_of(0, 0) + rs_got(0, 3, 0) + rs_got(1, 3, 0)
        got(XA.at[1], rxa.at[1])
        total = total + XA[1].astype(F32)
        AG[1, n_me, :, cols_of(0)] = (total * SL[:, cols_of(0)]).astype(BF)

    def rs_drain():
        for d in range(8):
            rc(XBs.at[d], XBr.at[d], rxb_s.at[d], rxb_r.at[d], partner).wait_send()
        rc(XA.at[0], XA.at[1], rxa.at[0], rxa.at[1], partner).wait_send()
        for s in range(4):
            for lane in range(3):
                for di in range(2):
                    src, dst = rs_refs(di, s, lane)
                    rc(src, dst, rz_s.at[di, s, lane], rz_r.at[di, s, lane], nbr[di]).wait_send()

    rs_start_x()
    rs_start_z(0)
    rs_start_z(1)
    ag_step(0, 3)
    rs_start_z(2)
    feature_pass(1)
    ag_last(0)
    rs_step(0)
    feature_end(1)
    for d in range(8):
        xb_got(0, d)

    def out_tile(t, _):
        rows = pl.ds(pl.multiple_of(t * 256, 256), 256)
        act = AG[0, :, :, rows].reshape(16 * B, 256)
        PO[rows, :] = dot(act, UI[0].reshape(16 * B, D), 0, 0).astype(BF)
        return 0

    lax.fori_loop(0, 2, out_tile, 0)
    rs_step(1)
    lax.fori_loop(2, 4, out_tile, 0)
    rs_step(2)
    lax.fori_loop(4, 6, out_tile, 0)
    ocopy_out = pltpu.make_async_copy(PO, gwout_o, o_sem.at[0])
    ocopy_out.start()
    rs_last()
    ag_start(1)
    wcopy_in.wait()
    ag_pair(1)

    offs = (0, 2, 6, 10, 14, 16)

    def blocks_of(h):
        if h in (0, 4):
            return [blk(0, h), blk(1, h)]
        return [blk(0, h), blk(0, -h), blk(1, h), blk(1, -h)]

    def gin_part(h):
        for d in sorted({h % 8, -h % 8}):
            xb_got(1, d)
        left = jnp.concatenate([AG[1, n] for n in blocks_of(h)], axis=0)
        m = offs[h + 1] - offs[h]
        slot = pl.ds(offs[h], m)
        theirs = WI[pl.ds(pl.multiple_of((1 - core) * HD, 128), HD), :]
        CS[0, slot] = dot(left, theirs, 1, 1).astype(BF).reshape(m, B, HD)
        rc(CS.at[0, slot], CS.at[1, slot], cs_s.at[h], cs_r.at[h], sib).start()
        mine = WI[pl.ds(pl.multiple_of(core * HD, 128), HD), :]
        Q[slot] = dot(left, mine, 1, 1).reshape(m, B, HD)

    def gin_send(h):
        m = offs[h + 1] - offs[h]
        slot = pl.ds(offs[h], m)
        got(CS.at[1, slot], cs_r.at[h])
        GO[slot] = (Q[slot] + CS[1, slot].astype(F32)).astype(BF)
        for i, n in enumerate(blocks_of(h)):
            at = offs[h] + i

            @pl.when(n == me_d)
            def _():
                GI[chip_d, core] = GO[at]

            @pl.when(n != me_d)
            def _():
                dev = (lax.div(n, 8), lax.rem(n, 8), col)
                rc(GO.at[at], GI.at[chip_d, core], gi_s.at[at], gi_r.at[me_d], dev).start()

    ag_step(1, 1)
    gin_part(0)
    ag_step(1, 2)
    gin_send(0)
    gin_part(1)
    ag_step(1, 3)
    gin_send(1)
    gin_part(2)
    ag_last(1)
    gin_send(2)
    gin_part(3)
    gin_part(4)
    gin_send(3)
    gin_send(4)

    def in_tile(t, _):
        cols = pl.ds(pl.multiple_of(t * 256, 256), 256)
        grad = AG[1, :, :, cols].reshape(16 * B, 256)
        PI[:, cols] = dot(UI[1].reshape(16 * B, D), grad, 0, 0).astype(BF)
        return 0

    lax.fori_loop(0, 6, in_tile, 0)
    ocopy_in = pltpu.make_async_copy(PI, gwin_o, o_sem.at[1])
    ocopy_in.start()

    def gi_wait(j, _):
        t = lax.rem(me_d + j, 16)
        got(GI.at[lax.div(t, 2), lax.rem(t, 2)], gi_r.at[t])
        return 0

    lax.fori_loop(1, 16, gi_wait, 0)
    for c in range(2):
        total = GI[0, c].astype(F32)
        for i in range(1, 8):
            total = total + GI[i, c].astype(F32)
        gin_o[:, c * HD:(c + 1) * HD] = total.astype(BF)

    for a in range(2):
        def sent(j, _):
            ref = UI.at[a, 0]
            rc(ref, ref, u_s.at[a, j], u_r.at[a, 0], sib).wait_send()
            return 0

        def passed(j, _):
            ref = UI.at[a, 0]
            rc(ref, ref, u_f.at[a, j], u_r.at[a, 0], sib).wait_send()
            return 0

        lax.fori_loop(1, 8, sent, 0)
        lax.fori_loop(0, 8, passed, 0)
        ag_drain(a)
    for k in range(2):
        @pl.when(jnp.logical_not(jnp.logical_and(dp == k, dp == xh)))
        def _():
            rc(pre.at[k], PRE.at[0], p_s.at[k], p_r.at[0], sib).wait_send()
    rs_drain()
    for h in range(5):
        slot = pl.ds(offs[h], offs[h + 1] - offs[h])
        rc(CS.at[0, slot], CS.at[1, slot], cs_s.at[h], cs_r.at[h], sib).wait_send()
        for i, n in enumerate(blocks_of(h)):
            @pl.when(n != me_d)
            def _():
                at = offs[h] + i
                rc(GO.at[at], GI.at[0, 0], gi_s.at[at], gi_r.at[0], sib).wait_send()
    ocopy_out.wait()
    ocopy_in.wait()


def body(inputs, upstream, preact, w_in, w_out):
    pre = jnp.pad(jnp.swapaxes(preact, 0, 1), ((0, 0), (0, 8), (0, 0)))
    vmem = pl.BlockSpec(memory_space=pltpu.VMEM)
    hbm = pl.BlockSpec(memory_space=pl.ANY)
    dma = pltpu.SemaphoreType.DMA
    grad_in, grad_w_in, grad_w_out = pl.pallas_call(
        kernel,
        out_shape=(
            jax.ShapeDtypeStruct((B, D), BF),
            jax.ShapeDtypeStruct((D, H), BF),
            jax.ShapeDtypeStruct((H, D), BF),
        ),
        in_specs=[vmem, vmem, vmem, hbm, hbm],
        out_specs=(vmem, hbm, hbm),
        scratch_shapes=[
            pltpu.VMEM((2, 16, B, D), BF),
            pltpu.VMEM((2, 16, B, H), BF),
            pltpu.VMEM((16, B, H), F32),
            pltpu.VMEM((D, H), BF),
            pltpu.VMEM((H, D), BF),
            pltpu.VMEM((2, 48, H), BF),
            pltpu.VMEM((B, H), F32),
            pltpu.VMEM((2, 4, 2, B, HA), BF),
            pltpu.VMEM((2, 4, 2, B, HA), BF),
            pltpu.VMEM((2, 4, B, HB), BF),
            pltpu.VMEM((2, 4, B, HB), BF),
            pltpu.VMEM((8, B, HB), BF),
            pltpu.VMEM((8, B, HB), BF),
            pltpu.VMEM((2, B, HA), BF),
            pltpu.VMEM((2, 16, B, HD), BF),
            pltpu.VMEM((16, B, HD), F32),
            pltpu.VMEM((16, B, HD), BF),
            pltpu.VMEM((8, 2, B, HD), BF),
            pltpu.VMEM((H, D), BF),
            pltpu.VMEM((D, H), BF),
            dma((2,)), dma((2,)), dma((2,)), dma((2,)),
            dma((2, 16)), dma((2, 8)), dma((2, 8)),
            dma((2, 2, 4, 3)), dma((2, 2, 4, 3)),
            dma((2,)), dma((2,)), dma((2, 8)), dma((2, 8)),
            dma((2, 4, 3)), dma((2, 4, 3)), dma((8,)), dma((8,)), dma((2,)),
            dma((5,)), dma((5,)), dma((16,)), dma((16,)),
        ],
        compiler_params=pltpu.CompilerParams(
            collective_id=0, has_side_effects=True, vmem_limit_bytes=60 * 2**20
        ),
        cost_estimate=pl.CostEstimate(
            flops=4 * 2 * 1280 * D * H, bytes_accessed=5 * 2 * D * H, transcendentals=B * H
        ),
    )(inputs, upstream, pre, w_in.reshape(D, H), w_out.reshape(H, D))
    return grad_in, grad_w_in.reshape(w_in.shape), grad_w_out.reshape(w_out.shape)


def solution(mesh):
    return jax.shard_map(
        body,
        mesh=mesh,
        in_specs=(
            P(("dp", "row"), "col"),
            P(("dp", "row"), "col"),
            P(("dp", "col"), None, "row"),
            P("col", "dp", "row"),
            P("dp", "row", "col"),
        ),
        out_specs=(P(("dp", "row"), "col"), P("col", "dp", "row"), P("dp", "row", "col")),
        check_vma=False,
    )
```

time: 762 us -> 163 us (0.21)
  waiting for transfers between devices: 671 us -> 0 us
  Pallas kernels: 0 us -> 154 us
  matrix products: 31.2 us -> 0 us
  blocking collectives: 26.5 us -> 0 us
  between operations: 14.2 us -> 0.64 us
    reduce_scatter x4 -> x0, waiting for transfers between devices: 387 us -> none  [the longest x1 225 us: body(): lax.psum_scatter(right_product(upstream_all, w_out_mat), 'col', scatter_d...]
    all_gather x4 -> x0, waiting for transfers between devices: 282 us -> none  [the longest x1 95.8 us: body(): lax.all_gather(grad_pre, 'col', axis=0, tiled=True)]
    pallas_call x0 -> x1, Pallas kernels: none -> 154 us  [body(): pl.pallas_call(kernel, out_shape=(jax.ShapeDtypeStruct((B, D), BF), jax.S...]
    dot_general x4 -> x0, matrix products: 31.2 us -> none  [the longest x2 15.7 us: right_product(): lax.dot_general(source, matrix, (((1,), (1,)), ((), ())), preferred_eleme...]
    all_gather x2 -> x0, blocking collectives: 26.5 us -> none  [the longest x1 13.9 us: body(): lax.all_gather(upstream, 'row', axis=0, tiled=True)]
  transfers between devices with their start and end apart: 8 -> 0, of which waited for: 8 -> 0; matrix products, arithmetic and copies ran while one was open for 5% -> 0% of each run, Pallas kernels for 0% -> 0%
where the time goes in v1:
time: 163 us
  Pallas kernels  154 us (94%)
  local copies, waits for them, and re-layouts  8.05 us (5%)
    pallas_call x1, Pallas kernels, body(): pl.pallas_call(kernel, out_shape=(jax.ShapeDtypeStruct((B, D), BF), jax.S...  154 us
    unnamed x6, local copies, waits for them, and re-layouts  7.31 us

profile of v1, /device:TPU:16, one launch (start us, length us, event | category | flops | bytes accessed | tf_op | source)
XLA Modules:
  0.0 163.0 jit_solution(11462109285365704199)
XLA Ops:
  0.6 1.0 copy.10
  1.6 0.7 pad.4.pre
  2.3 154.3 %shard_map.76 = (bf16[80,768]{1,0:T(8,128)(2,1)}, bf16[768,1536]{1,0:T(8,128)(2,1)}, bf16[1536,768]{1,0:T(8,128)(2,1)}) custom-call(bf16[80,768]{1,0:T(8,128)(2,1)} %inp.1, bf16[80,768]{1,0:T(8,128)(2,1)} %ups.1, bf16[2,48,1536]{2,1,0:T(8,128)(2,1)} %pad.4.pre, bf16[768,1536]{1,0:T(8,128)(2,1)} %bitcast.10, bf16[1536,768]{1,0:T(8,128)(2,1)} %bitcast.11), custom_call_target="tpu_custom_call" | custom-call | flops 12079595520 | bytes 11796480 | tf_op jit(solution)/shard_map/pallas_call | solution.py:443
  156.7 1.6 copy.14
  158.2 0.0 copy-start
  158.2 3.4 %copy.15 = bf16[768,1,1536]{2,0,1:T(8,128)(2,1)} copy(bf16[768,1,1536]{2,0,1:T(8,128)(2,1)} %bitcast.8) | data formatting | bytes 4718592
  161.6 0.0 copy-done
  161.6 1.4 copy.16
Async XLA Ops:
  158.2 3.4 %copy-start = (bf16[1536,768]{1,0:T(8,128)(2,1)S(1)}, bf16[1536,768]{1,0:T(8,128)(2,1)}, u32[]{:S(2)}) copy-start(bf16[1536,768]{1,0:T(8,128)(2,1)} %get-tuple-element.8) | copy-start | bytes 7077892

commit v2 on v1

v2 whole, which is shorter than its diff:
```python
import functools

import jax
import jax.numpy as jnp
from jax import lax
from jax.experimental import pallas as pl
from jax.experimental.pallas import tpu as pltpu
from jax.sharding import PartitionSpec as P

GELU_C = 0.7978845608028654
GELU_K = 0.044715
MESH = pl.DeviceIdType.MESH
BF = jnp.bfloat16
F32 = jnp.float32

B = 80
D = 768
H = 1536
CUT = (768, 768)
HA = 768
HB = H - HA
HD = D // 2
SIGN = (1, -1)


def gelu_parts(wide):
    inner = jnp.tanh(GELU_C * (wide + GELU_K * wide * wide * wide))
    active = 0.5 * wide * (1.0 + inner)
    slope = 0.5 * (1.0 + inner) + 0.5 * wide * (1.0 - inner * inner) * GELU_C * (
        1.0 + 3.0 * GELU_K * wide * wide
    )
    return active, slope


def dot(a, b, ca, cb):
    return lax.dot_general(a, b, (((ca,), (cb,)), ((), ())), preferred_element_type=F32)


def cols_of(lane, cut):
    return pl.ds(0, cut) if lane < 2 else pl.ds(cut, H - cut)


def half_of(lane, part, cut):
    start, size = (0, cut // 2) if lane < 2 else (cut, (H - cut) // 2)
    return pl.ds(start + part * size, size)


def kernel(
    inp, ups, pre, w_in, w_out,
    gin_o, gwin_o, gwout_o,
    UI, AG, PB, ACC, WI, WO, PRE, SL, RA, SA, RB, SB, XBr, XBs, XA, CS, Q, GO, GI,
    w_sem, p_r, p_s, u_r, u_s, u_f, z_r, z_s, xa_r, xa_s, xb_r, xb_s,
    rz_r, rz_s, rxb_r, rxb_s, rxa, cs_r, cs_s, gi_r, gi_s,
):
    dp, row, col = lax.axis_index("dp"), lax.axis_index("row"), lax.axis_index("col")
    y, core = lax.div(row, 2), lax.rem(row, 2)
    z, xh = lax.div(col, 2), lax.rem(col, 2)
    xo = 1 - xh
    me_d = dp * 8 + row
    chip_d = dp * 4 + y
    n_me = xh * 8 + z

    def zrel(d):
        return lax.rem(z + (d + 8), 8)

    def blk(lane, d):
        return (xo if lane == 1 else xh) * 8 + zrel(d)

    nbr = tuple((dp, row, zrel(s) * 2 + xh) for s in SIGN)
    partner = (dp, row, z * 2 + xo)
    sib = (dp, y * 2 + (1 - core), col)

    def rc(src, dst, ss, rs, dev):
        return pltpu.make_async_remote_copy(
            src_ref=src, dst_ref=dst, send_sem=ss, recv_sem=rs, device_id=dev, device_id_type=MESH
        )

    def got(ref, sem):
        pltpu.make_async_copy(ref, ref, sem).wait()

    wcopy_out = pltpu.make_async_copy(w_out, WO, w_sem.at[0])
    wcopy_in = pltpu.make_async_copy(w_in, WI, w_sem.at[1])
    wcopy_out.start()
    wcopy_in.start()

    barrier = pltpu.get_barrier_semaphore()

    def greet(dev):
        pl.semaphore_signal(barrier, inc=1, device_id=dev, device_id_type=MESH)

    def greet_group(j, _):
        t = lax.rem(me_d + j, 16)
        greet((lax.div(t, 8), lax.rem(t, 8), col))
        return 0

    lax.fori_loop(1, 16, greet_group, 0)
    greet(nbr[0])
    greet(nbr[1])
    greet(partner)
    greet((1 - dp, row, z * 2 + xo))
    UI[0, me_d] = ups[...]
    UI[1, me_d] = inp[...]
    pl.semaphore_wait(barrier, 19)

    dpp = (1 - dp, row, col)
    me_o = (1 - dp) * 8 + row

    def peer(j):
        return lax.rem(y + j, 4) * 2 + core

    def share(a, n, at):
        ref = UI.at[a, n]
        for j in range(1, 4):
            rc(ref, ref, u_s.at[a, at + j], u_r.at[a, n], (dp, peer(j), col)).start()
        rc(ref, ref, u_f.at[a, at], u_r.at[a, n], sib).start()

    def feature_start(a):
        ref = UI.at[a, me_d]
        rc(ref, ref, u_s.at[a, 0], u_r.at[a, me_d], dpp).start()
        share(a, me_d, 0)

    def feature_dp(a):
        got(UI.at[a, me_o], u_r.at[a, me_o])
        share(a, me_o, 4)

    def feature_pass(a):
        for j in range(1, 4):
            for i, g in enumerate((dp, 1 - dp)):
                n = g * 8 + peer(4 - j)
                ref = UI.at[a, n]
                got(ref, u_r.at[a, n])
                rc(ref, ref, u_f.at[a, i * 4 + j], u_r.at[a, n], sib).start()

    def feature_end(a):
        def step(j, _):
            n = j * 2 + (1 - core)
            got(UI.at[a, n], u_r.at[a, n])
            return 0

        lax.fori_loop(0, 8, step, 0)

    def feature_drain(a):
        ref = UI.at[a, 0]
        for j in (0, 1, 2, 3, 5, 6, 7):
            rc(ref, ref, u_s.at[a, j], u_r.at[a, 0], sib).wait_send()
        for j in range(8):
            rc(ref, ref, u_f.at[a, j], u_r.at[a, 0], sib).wait_send()

    for k in range(2):
        own = jnp.logical_and(dp == k, dp == xh)
        src, dst = pre.at[k], PRE.at[xh]

        @pl.when(own)
        def _():
            pltpu.make_async_copy(src, dst, p_r.at[xh]).start()

        @pl.when(jnp.logical_not(own))
        def _():
            rc(src, dst, p_s.at[k], p_r.at[xh], (k, row, z * 2 + dp)).start()

    feature_start(0)

    got(PRE.at[0], p_r.at[0])
    got(PRE.at[1], p_r.at[1])
    wide = jnp.concatenate([PRE[0].astype(F32), PRE[1].astype(F32)], axis=0)
    active, slope = gelu_parts(wide)
    AG[0, n_me] = active.astype(BF)
    SL[...] = slope

    def z_send(a, di, h, lane, d):
        cols = cols_of(lane, CUT[a]) if h < 4 else half_of(lane, di, CUT[a])
        ref = AG.at[a, blk(lane, d), :, cols]
        rc(ref, ref, z_s.at[a, di, h - 1, lane], z_r.at[a, di, h - 1, lane], nbr[di]).start()

    def z_got(a, di, h, lane, d):
        cols = cols_of(lane, CUT[a]) if h < 4 else half_of(lane, di, CUT[a])
        got(AG.at[a, blk(lane, d), :, cols], z_r.at[a, di, h - 1, lane])

    def xb_send(a, d):
        ref = AG.at[a, blk(2, d), :, cols_of(2, CUT[a])]
        rc(ref, ref, xb_s.at[a, d % 8], xb_r.at[a, d % 8], partner).start()

    def xb_got(a, d):
        got(AG.at[a, blk(1, d), :, cols_of(2, CUT[a])], xb_r.at[a, d % 8])

    def ag_start(a, lane):
        if lane == 0:
            ref = AG.at[a, n_me, :, cols_of(0, CUT[a])]
            rc(ref, ref, xa_s.at[a], xa_r.at[a], partner).start()
        for di in range(2):
            z_send(a, di, 1, lane, 0)
        if lane == 2:
            xb_send(a, 0)

    def ag_pair(a):
        got(AG.at[a, xo * 8 + z, :, cols_of(1, CUT[a])], xa_r.at[a])
        for di in range(2):
            z_send(a, di, 1, 1, 0)

    def ag_step(a, h, lanes=(0, 2, 1), take=True, pass_z=True, pass_x=True):
        for lane in lanes:
            for di, s in enumerate(SIGN):
                if take:
                    z_got(a, di, h, lane, -s * h)
                if pass_z:
                    z_send(a, di, h + 1, lane, -s * h)
                if lane == 2 and pass_x:
                    xb_send(a, -s * h)

    def ag_last(a):
        for lane in (2, 0, 1):
            for di, s in enumerate(SIGN):
                z_got(a, di, 4, lane, -s * 4)
            if lane == 2:
                xb_send(a, 4)

    def ag_drain(a):
        rc(AG.at[a, 0, :, cols_of(0, CUT[a])], AG.at[a, 0, :, cols_of(0, CUT[a])], xa_s.at[a], xa_r.at[a], partner).wait_send()
        for d in range(8):
            ref = AG.at[a, 0, :, cols_of(2, CUT[a])]
            rc(ref, ref, xb_s.at[a, d], xb_r.at[a, d], partner).wait_send()
        for h in range(1, 5):
            for lane in range(3):
                for di in range(2):
                    ref = AG.at[a, 0, :, cols_of(lane, CUT[a]) if h < 4 else half_of(lane, di, CUT[a])]
                    rc(ref, ref, z_s.at[a, di, h - 1, lane], z_r.at[a, di, h - 1, lane], nbr[di]).wait_send()

    ag_start(0, 0)
    ag_start(0, 2)
    feature_dp(0)
    ag_pair(0)
    feature_pass(0)
    ag_step(0, 1)
    feature_end(0)
    feature_start(1)
    wcopy_out.wait()

    def blocks_of(h):
        if h in (0, 4):
            return [blk(0, h), blk(1, h)]
        return [blk(0, h), blk(0, -h), blk(1, h), blk(1, -h)]

    def rows_of(n):
        return pl.ds(pl.multiple_of(n * B, 16), B)

    def back_part(h):
        blocks = blocks_of(h)
        left = jnp.concatenate([UI[0, n] for n in blocks], axis=0)

        def tile(t, _):
            cols = pl.ds(pl.multiple_of(t * 256, 256), 256)
            part = dot(left, WO[cols, :], 1, 1)
            for i, n in enumerate(blocks):
                PB[rows_of(n), cols] = part[i * B:(i + 1) * B]
            return 0

        lax.fori_loop(0, 6, tile, 0)

    def rs_refs(di, s, lane):
        if lane < 2:
            cols = slice(None) if s else pl.ds(di * (HA // 2), HA // 2)
            return SA.at[di, s, lane, :, cols], RA.at[di, s, lane, :, cols]
        cols = slice(None) if s else pl.ds(di * (HB // 2), HB // 2)
        return SB.at[di, s, :, cols], RB.at[di, s, :, cols]

    def rs_send(di, s, lane):
        src, dst = rs_refs(di, s, lane)
        rc(src, dst, rz_s.at[di, s, lane], rz_r.at[di, s, lane], nbr[di]).start()

    def rs_got(di, s, lane):
        dst = rs_refs(di, s, lane)[1]
        got(dst, rz_r.at[di, s, lane])
        return dst[...].astype(F32)

    def part_of(lane, d):
        if lane < 2:
            return PB[rows_of(blk(lane, d)), cols_of(lane, HA)]
        got(XBr.at[d % 8], rxb_r.at[d % 8])
        return PB[rows_of(blk(lane, d)), cols_of(2, HA)] + XBr[d % 8].astype(F32)

    def rs_start_x(h):
        for d in sorted({h % 8, -h % 8}):
            XBs[d] = PB[rows_of(blk(1, d)), cols_of(2, HA)].astype(BF)
            rc(XBs.at[d], XBr.at[d], rxb_s.at[d], rxb_r.at[d], partner).start()

    def rs_start_z(lane):
        val = part_of(lane, 4)
        for di in range(2):
            src = rs_refs(di, 0, lane)[0]
            width = (HA if lane < 2 else HB) // 2
            src[...] = val[:, di * width:(di + 1) * width].astype(BF)
            rs_send(di, 0, lane)

    def rs_step(s, *lanes):
        for lane in lanes:
            for di, sg in enumerate(SIGN):
                come = rs_got(di, s, lane)
                val = part_of(lane, sg * (3 - s))
                full = rs_refs(di, s + 1, lane)[0]
                if s == 0:
                    width = val.shape[1] // 2
                    halves = [val[:, :width], val[:, width:]]
                    halves[di] = halves[di] + come
                    val = jnp.concatenate(halves, axis=1)
                else:
                    val = val + come
                full[...] = val.astype(BF)
                rs_send(di, s + 1, lane)

    def rs_last_far():
        other = part_of(1, 0) + rs_got(0, 3, 1) + rs_got(1, 3, 1)
        XA[0] = other.astype(BF)
        rc(XA.at[0], XA.at[1], rxa.at[0], rxa.at[1], partner).start()

    def rs_last_near():
        total = part_of(0, 0) + rs_got(0, 3, 0) + rs_got(1, 3, 0)
        got(XA.at[1], rxa.at[1])
        total = total + XA[1].astype(F32)
        AG[1, n_me, :, cols_of(0, HA)] = (total * SL[:, cols_of(0, HA)]).astype(BF)

    def rs_last_x():
        total = part_of(2, 0) + rs_got(0, 3, 2) + rs_got(1, 3, 2)
        AG[1, n_me, :, cols_of(2, HA)] = (total * SL[:, cols_of(2, HA)]).astype(BF)

    def rs_drain():
        for d in range(8):
            rc(XBs.at[d], XBr.at[d], rxb_s.at[d], rxb_r.at[d], partner).wait_send()
        rc(XA.at[0], XA.at[1], rxa.at[0], rxa.at[1], partner).wait_send()
        for s in range(4):
            for lane in range(3):
                for di in range(2):
                    src, dst = rs_refs(di, s, lane)
                    rc(src, dst, rz_s.at[di, s, lane], rz_r.at[di, s, lane], nbr[di]).wait_send()

    def out_part(sets, first, end):
        blocks = [n for h in sets for n in blocks_of(h)]
        right = jnp.concatenate([UI[0, n] for n in blocks], axis=0)

        def tile(t, _):
            rows = pl.ds(pl.multiple_of(t * 256, 256), 256)
            left = jnp.concatenate([AG[0, n, :, rows] for n in blocks], axis=0)
            part = dot(left, right, 0, 0)
            if 4 in sets:
                gwout_o[rows, :] = (ACC[rows, :] + part).astype(BF)
            else:
                ACC[rows, :] = part
            return 0

        lax.fori_loop(first, end, tile, 0)

    def in_part(sets, first, end):
        blocks = [n for h in sets for n in blocks_of(h)]
        left = jnp.concatenate([UI[1, n] for n in blocks], axis=0)

        def tile(t, _):
            cols = pl.ds(pl.multiple_of(t * 256, 256), 256)
            right = jnp.concatenate([AG[1, n, :, cols] for n in blocks], axis=0)
            part = dot(left, right, 0, 0)
            if 4 in sets:
                gwin_o[:, cols] = (PB[:D, cols] + part).astype(BF)
            elif 0 in sets:
                PB[:D, cols] = part
            else:
                PB[:D, cols] += part
            return 0

        lax.fori_loop(first, end, tile, 0)

    offs = (0, 2, 6, 10, 14, 16)

    def gin_part(h):
        for d in sorted({h % 8, -h % 8}):
            xb_got(1, d)
        left = jnp.concatenate([AG[1, n] for n in blocks_of(h)], axis=0)
        m = offs[h + 1] - offs[h]
        slot = pl.ds(offs[h], m)
        theirs = WI[pl.ds(pl.multiple_of((1 - core) * HD, 128), HD), :]
        CS[0, slot] = dot(left, theirs, 1, 1).astype(BF).reshape(m, B, HD)
        rc(CS.at[0, slot], CS.at[1, slot], cs_s.at[h], cs_r.at[h], sib).start()
        mine = WI[pl.ds(pl.multiple_of(core * HD, 128), HD), :]
        Q[slot] = dot(left, mine, 1, 1).reshape(m, B, HD)

    def gin_send(h):
        m = offs[h + 1] - offs[h]
        slot = pl.ds(offs[h], m)
        got(CS.at[1, slot], cs_r.at[h])
        GO[slot] = (Q[slot] + CS[1, slot].astype(F32)).astype(BF)
        for i, n in enumerate(blocks_of(h)):
            at = offs[h] + i

            @pl.when(n == me_d)
            def _():
                GI[chip_d, core] = GO[at]

            @pl.when(n != me_d)
            def _():
                dev = (lax.div(n, 8), lax.rem(n, 8), col)
                rc(GO.at[at], GI.at[chip_d, core], gi_s.at[at], gi_r.at[me_d], dev).start()

    back_part(4)
    rs_start_x(4)
    rs_start_z(0)
    rs_start_z(1)
    back_part(3)
    rs_start_x(3)
    back_part(2)
    rs_start_x(2)
    back_part(1)
    rs_start_x(1)
    back_part(0)
    rs_start_x(0)
    rs_step(0, 0, 1)
    rs_start_z(2)
    feature_dp(1)
    rs_step(1, 0, 1)
    rs_step(0, 2)
    feature_pass(1)
    rs_step(2, 0, 1)
    rs_step(1, 2)
    ag_step(0, 2, (0,))
    rs_last_far()
    rs_step(2, 2)
    ag_step(0, 2, (2, 1))
    rs_last_near()
    ag_start(1, 0)
    rs_last_x()
    ag_start(1, 2)
    wcopy_in.wait()
    feature_end(1)
    feature_drain(0)
    feature_drain(1)
    rs_drain()
    ag_pair(1)
    ag_step(1, 1)
    ag_step(0, 3, pass_z=False)
    gin_part(0)
    for d in (0, 1, 7, 2, 6):
        xb_got(0, d)
    out_part((0, 1, 2), 0, 6)
    ag_step(1, 2)
    gin_send(0)
    gin_part(1)
    in_part((0, 1), 0, 6)
    ag_step(1, 3)
    ag_step(0, 3, take=False, pass_x=False)
    gin_send(1)
    gin_part(2)
    in_part((2,), 0, 6)
    ag_last(1)
    gin_send(2)
    gin_part(3)
    gin_part(4)
    ag_last(0)
    gin_send(3)
    in_part((3, 4), 0, 3)
    gin_send(4)
    in_part((3, 4), 3, 6)
    for d in (3, 5, 4):
        xb_got(0, d)
    out_part((3, 4), 0, 6)
    ag_drain(0)

    def gi_wait(j, _):
        t = lax.rem(me_d + j, 16)
        got(GI.at[lax.div(t, 2), lax.rem(t, 2)], gi_r.at[t])
        return 0

    lax.fori_loop(1, 16, gi_wait, 0)

    def gin_sum(i, _):
        rows = pl.ds(pl.multiple_of(i * 16, 16), 16)
        for c in range(2):
            total = GI[0, c, rows].astype(F32)
            for j in range(1, 8):
                total = total + GI[j, c, rows].astype(F32)
            gin_o[rows, c * HD:(c + 1) * HD] = total.astype(BF)
        return 0

    lax.fori_loop(0, 5, gin_sum, 0)

    ag_drain(1)
    for k in range(2):
        @pl.when(jnp.logical_not(jnp.logical_and(dp == k, dp == xh)))
        def _():
            rc(pre.at[k], PRE.at[0], p_s.at[k], p_r.at[0], sib).wait_send()
    for h in range(5):
        slot = pl.ds(offs[h], offs[h + 1] - offs[h])
        rc(CS.at[0, slot], CS.at[1, slot], cs_s.at[h], cs_r.at[h], sib).wait_send()
        for i, n in enumerate(blocks_of(h)):
            @pl.when(n != me_d)
            def _():
                at = offs[h] + i
                rc(GO.at[at], GI.at[0, 0], gi_s.at[at], gi_r.at[0], sib).wait_send()


def body(inputs, upstream, preact, w_in, w_out):
    pre = jnp.swapaxes(preact, 0, 1)
    vmem = pl.BlockSpec(memory_space=pltpu.VMEM)
    hbm = pl.BlockSpec(memory_space=pl.ANY)
    dma = pltpu.SemaphoreType.DMA
    grad_in, grad_w_in, grad_w_out = pl.pallas_call(
        kernel,
        out_shape=(
            jax.ShapeDtypeStruct((B, D), BF),
            pltpu.VMEM((D, H), BF),
            pltpu.VMEM((H, D), BF),
        ),
        in_specs=[vmem, vmem, vmem, hbm, hbm],
        out_specs=(vmem, vmem, vmem),
        scratch_shapes=[
            pltpu.VMEM((2, 16, B, D), BF),
            pltpu.VMEM((2, 16, B, H), BF),
            pltpu.VMEM((16 * B, H), F32),
            pltpu.VMEM((H, D), F32),
            pltpu.VMEM((D, H), BF),
            pltpu.VMEM((H, D), BF),
            pltpu.VMEM((2, 40, H), BF),
            pltpu.VMEM((B, H), F32),
            pltpu.VMEM((2, 4, 2, B, HA), BF),
            pltpu.VMEM((2, 4, 2, B, HA), BF),
            pltpu.VMEM((2, 4, B, HB), BF),
            pltpu.VMEM((2, 4, B, HB), BF),
            pltpu.VMEM((8, B, HB), BF),
            pltpu.VMEM((8, B, HB), BF),
            pltpu.VMEM((2, B, HA), BF),
            pltpu.VMEM((2, 16, B, HD), BF),
            pltpu.VMEM((16, B, HD), F32),
            pltpu.VMEM((16, B, HD), BF),
            pltpu.VMEM((8, 2, B, HD), BF),
            dma((2,)), dma((2,)), dma((2,)),
            dma((2, 16)), dma((2, 8)), dma((2, 8)),
            dma((2, 2, 4, 3)), dma((2, 2, 4, 3)),
            dma((2,)), dma((2,)), dma((2, 8)), dma((2, 8)),
            dma((2, 4, 3)), dma((2, 4, 3)), dma((8,)), dma((8,)), dma((2,)),
            dma((5,)), dma((5,)), dma((16,)), dma((16,)),
        ],
        compiler_params=pltpu.CompilerParams(
            collective_id=0, has_side_effects=True, vmem_limit_bytes=56 * 2**20
        ),
        cost_estimate=pl.CostEstimate(
            flops=4 * 2 * 1280 * D * H, bytes_accessed=5 * 2 * D * H, transcendentals=B * H
        ),
    )(inputs, upstream, pre, w_in.reshape(D, H), w_out.reshape(H, D))
    return grad_in, grad_w_in.reshape(w_in.shape), grad_w_out.reshape(w_out.shape)


def solution(mesh):
    return jax.shard_map(
        body,
        mesh=mesh,
        in_specs=(
            P(("dp", "row"), "col"),
            P(("dp", "row"), "col"),
            P(("dp", "col"), None, "row"),
            P("col", "dp", "row"),
            P("dp", "row", "col"),
        ),
        out_specs=(P(("dp", "row"), "col"), P("col", "dp", "row"), P("dp", "row", "col")),
        check_vma=False,
    )
```

time: 163 us -> 128 us (0.79)
  Pallas kernels: 154 us -> 122 us
  local copies, waits for them, and re-layouts: 8.05 us -> 5.13 us
    pallas_call x1, Pallas kernels: 154 us -> 122 us  [body(): pl.pallas_call(kernel, out_shape=(jax.ShapeDtypeStruct((B, D), BF), pltpu...]
    unnamed x6, local copies, waits for them, and re-layouts: 7.31 us -> 5.13 us
where the time goes in v2:
time: 128 us
  Pallas kernels  122 us (95%)
  local copies, waits for them, and re-layouts  5.13 us (4%)
    pallas_call x1, Pallas kernels, body(): pl.pallas_call(kernel, out_shape=(jax.ShapeDtypeStruct((B, D), BF), pltpu...  122 us
    unnamed x6, local copies, waits for them, and re-layouts  5.13 us

profile of v2, /device:TPU:16, one launch (start us, length us, event | category | flops | bytes accessed | tf_op | source)
XLA Modules:
  0.0 127.9 jit_solution(7324145682098534723)
XLA Ops:
  0.6 1.7 %copy.10 = bf16[40,2,1536]{2,0,1:T(8,128)(2,1)} copy(bf16[40,2,1536]{2,1,0:T(2,128)(2,1)} %param.7) | data formatting | bytes 491520 | tf_op args[2]
  2.3 122.2 %shard_map.76 = (bf16[80,768]{1,0:T(8,128)(2,1)}, bf16[768,1536]{1,0:T(8,128)(2,1)S(1)}, bf16[1536,768]{1,0:T(8,128)(2,1)S(1)}) custom-call(bf16[80,768]{1,0:T(8,128)(2,1)} %inp.1, bf16[80,768]{1,0:T(8,128)(2,1)} %ups.1, bf16[2,40,1536]{2,1,0:T(8,128)(2,1)} %bitcast.9, bf16[768,1536]{1,0:T(8,128)(2,1)} %bitcast.10, bf16[1536,768]{1,0:T(8,128)(2,1)} %bitcast.11), custom_call_target="tpu_custom_call" | custom-call | flops 12079595520 | bytes 11796480 | tf_op jit(solution)/shard_map/pallas_call | solution.py:501
  124.5 1.4 %copy.14 = bf16[768,1,1536]{2,0,1:T(8,128)(2,1)} copy(bf16[768,1,1536]{2,0,1:T(8,128)(2,1)S(1)} %bitcast.8) | data formatting | bytes 4718592
  125.9 0.0 copy-start
  125.9 1.4 %copy.15 = bf16[1,1536,768]{2,1,0:T(8,128)(2,1)} copy(bf16[1,1536,768]{2,1,0:T(8,128)(2,1)S(1)} %bitcast.7) | data formatting | bytes 4718592
  127.3 0.0 copy-done
  127.3 0.6 copy.16
Async XLA Ops:
  125.9 1.4 %copy-start = (bf16[80,768]{1,0:T(8,128)(2,1)S(1)}, bf16[80,768]{1,0:T(8,128)(2,1)}, u32[]{:S(2)}) copy-start(bf16[80,768]{1,0:T(8,128)(2,1)} %get-tuple-element.15) | copy-start | bytes 368644

commit v3 on v2

--- a/solution.py
+++ b/solution.py
@@ -48,9 +48,9 @@
 def kernel(
     inp, ups, pre, w_in, w_out,
     gin_o, gwin_o, gwout_o,
-    UI, AG, PB, ACC, WI, WO, PRE, SL, RA, SA, RB, SB, XBr, XBs, XA, CS, Q, GO, GI,
+    UI, AG, PB, ACC, WI, WO, PV, PK, PRE, SL, RA, SA, RB, SB, XBr, XBs, XA, CS, Q, GO, GI, RX,
     w_sem, p_r, p_s, u_r, u_s, u_f, z_r, z_s, xa_r, xa_s, xb_r, xb_s,
-    rz_r, rz_s, rxb_r, rxb_s, rxa, cs_r, cs_s, gi_r, gi_s,
+    rz_r, rz_s, rxb_r, rxb_s, rxa, cs_r, cs_s, gi_r, gi_s, rx_r, rx_s,
 ):
     dp, row, col = lax.axis_index("dp"), lax.axis_index("row"), lax.axis_index("col")
     y, core = lax.div(row, 2), lax.rem(row, 2)
@@ -80,8 +80,6 @@
 
     wcopy_out = pltpu.make_async_copy(w_out, WO, w_sem.at[0])
     wcopy_in = pltpu.make_async_copy(w_in, WI, w_sem.at[1])
-    wcopy_out.start()
-    wcopy_in.start()
 
     barrier = pltpu.get_barrier_semaphore()
 
@@ -98,8 +96,19 @@
     greet(nbr[1])
     greet(partner)
     greet((1 - dp, row, z * 2 + xo))
-    UI[0, me_d] = ups[...]
-    UI[1, me_d] = inp[...]
+    own_copies = [
+        pltpu.make_async_copy(ref, UI.at[a, me_d], w_sem.at[2 + a]) for a, ref in enumerate((ups, inp))
+    ]
+    own_copies.append(pltpu.make_async_copy(pre, PV, w_sem.at[4]))
+    for copy in own_copies:
+        copy.start()
+    wcopy_out.start()
+    wcopy_in.start()
+    for copy in own_copies:
+        copy.wait()
+    both = PV[...]
+    for k in range(2):
+        PK[k] = both[:, k, :]
     pl.semaphore_wait(barrier, 19)
 
     dpp = (1 - dp, row, col)
@@ -146,26 +155,30 @@
         for j in range(8):
             rc(ref, ref, u_f.at[a, j], u_r.at[a, 0], sib).wait_send()
 
-    for k in range(2):
-        own = jnp.logical_and(dp == k, dp == xh)
-        src, dst = pre.at[k], PRE.at[xh]
-
-        @pl.when(own)
-        def _():
-            pltpu.make_async_copy(src, dst, p_r.at[xh]).start()
-
-        @pl.when(jnp.logical_not(own))
-        def _():
-            rc(src, dst, p_s.at[k], p_r.at[xh], (k, row, z * 2 + dp)).start()
+    groups = (cols_of(0, CUT[0]), cols_of(2, CUT[0]))
+    for c, cols in enumerate(groups):
+        for k in range(2):
+            own = jnp.logical_and(dp == k, dp == xh)
+            src, dst = PK.at[k, :, cols], PRE.at[xh, :, cols]
+
+            @pl.when(own)
+            def _():
+                pltpu.make_async_copy(src, dst, p_r.at[c, xh]).start()
+
+            @pl.when(jnp.logical_not(own))
+            def _():
+                rc(src, dst, p_s.at[c, k], p_r.at[c, xh], (k, row, z * 2 + dp)).start()
 
     feature_start(0)
 
-    got(PRE.at[0], p_r.at[0])
-    got(PRE.at[1], p_r.at[1])
-    wide = jnp.concatenate([PRE[0].astype(F32), PRE[1].astype(F32)], axis=0)
-    active, slope = gelu_parts(wide)
-    AG[0, n_me] = active.astype(BF)
-    SL[...] = slope
+    def act_part(c):
+        cols = groups[c]
+        for i in range(2):
+            got(PRE.at[i, :, cols], p_r.at[c, i])
+        wide = jnp.concatenate([PRE[0, :, cols].astype(F32), PRE[1, :, cols].astype(F32)], axis=0)
+        active, slope = gelu_parts(wide)
+        AG[0, n_me, :, cols] = active.astype(BF)
+        SL[:, cols] = slope
 
     def z_send(a, di, h, lane, d):
         cols = cols_of(lane, CUT[a]) if h < 4 else half_of(lane, di, CUT[a])
@@ -197,7 +210,7 @@
         for di in range(2):
             z_send(a, di, 1, 1, 0)
 
-    def ag_step(a, h, lanes=(0, 2, 1), take=True, pass_z=True, pass_x=True):
+    def ag_step(a, h, lanes=(2, 0, 1), take=True, pass_z=True, pass_x=True):
         for lane in lanes:
             for di, s in enumerate(SIGN):
                 if take:
@@ -207,8 +220,8 @@
                 if lane == 2 and pass_x:
                     xb_send(a, -s * h)
 
-    def ag_last(a):
-        for lane in (2, 0, 1):
+    def ag_last(a, lanes=(2, 0, 1)):
+        for lane in lanes:
             for di, s in enumerate(SIGN):
                 z_got(a, di, 4, lane, -s * 4)
             if lane == 2:
@@ -225,12 +238,16 @@
                     ref = AG.at[a, 0, :, cols_of(lane, CUT[a]) if h < 4 else half_of(lane, di, CUT[a])]
                     rc(ref, ref, z_s.at[a, di, h - 1, lane], z_r.at[a, di, h - 1, lane], nbr[di]).wait_send()
 
+    act_part(0)
     ag_start(0, 0)
+    act_part(1)
     ag_start(0, 2)
     feature_dp(0)
     ag_pair(0)
+    ag_step(0, 1, (0,))
     feature_pass(0)
-    ag_step(0, 1)
+    ag_step(0, 1, (2,), pass_x=False)
+    xb_send(0, -1)
     feature_end(0)
     feature_start(1)
     wcopy_out.wait()
@@ -243,8 +260,8 @@
     def rows_of(n):
         return pl.ds(pl.multiple_of(n * B, 16), B)
 
-    def back_part(h):
-        blocks = blocks_of(h)
+    def back_part(*sets):
+        blocks = [n for h in sets for n in blocks_of(h)]
         left = jnp.concatenate([UI[0, n] for n in blocks], axis=0)
 
         def tile(t, _):
@@ -368,6 +385,81 @@
 
     offs = (0, 2, 6, 10, 14, 16)
 
+    def gin_targets(h):
+        targets = []
+        for i, n in enumerate(blocks_of(h)):
+            g, r = lax.div(n, 8), lax.rem(n, 8)
+            slot = jnp.where(g == dp, 0, 1)
+            to = g if h >= 3 else dp
+            own = jnp.logical_and(r == row, to == dp)
+            targets.append((offs[h] + i, (to, r, col), slot, own))
+        return targets
+
+    away = lax.rem(row + 8 - z, 8)
+    direct = jnp.logical_and(away >= 3, away <= 5)
+
+    def gi_wait(slot):
+        def one(j, _):
+            yy, c = lax.div(j, 2), lax.rem(j, 2)
+            own = jnp.logical_and(j == row, jnp.logical_not(jnp.logical_and(direct, slot == 1)))
+
+            @pl.when(jnp.logical_not(own))
+            def _():
+                got(GI.at[slot, yy, c], gi_r.at[slot, yy, c])
+
+            return 0
+
+        lax.fori_loop(0, 8, one, 0)
+
+    def gi_rows(i, slot):
+        rows = pl.ds(pl.multiple_of(i * 16, 16), 16)
+        sums = []
+        for c in range(2):
+            total = GI[slot, 0, c, rows].astype(F32)
+            for j in range(1, 4):
+                total = total + GI[slot, j, c, rows].astype(F32)
+            sums.append(total)
+        return rows, jnp.concatenate(sums, axis=1)
+
+    def gin_relay():
+        @pl.when(jnp.logical_not(direct))
+        def _():
+            gi_wait(1)
+
+            def step(i, _):
+                rows, total = gi_rows(i, 1)
+                RX[0, rows] = total.astype(BF)
+                return 0
+
+            lax.fori_loop(0, 5, step, 0)
+            rc(RX.at[0], RX.at[1], rx_s.at[0], rx_r.at[0], dpp).start()
+
+    def gin_final():
+        gi_wait(0)
+
+        @pl.when(direct)
+        def _():
+            gi_wait(1)
+
+            def step(i, _):
+                rows, total = gi_rows(i, 0)
+                gin_o[rows] = (total + gi_rows(i, 1)[1]).astype(BF)
+                return 0
+
+            lax.fori_loop(0, 5, step, 0)
+
+        @pl.when(jnp.logical_not(direct))
+        def _():
+            got(RX.at[1], rx_r.at[0])
+
+            def step(i, _):
+                rows, total = gi_rows(i, 0)
+                gin_o[rows] = (total + RX[1, rows].astype(F32)).astype(BF)
+                return 0
+
+            lax.fori_loop(0, 5, step, 0)
+            rc(RX.at[0], RX.at[1], rx_s.at[0], rx_r.at[0], dpp).wait_send()
+
     def gin_part(h):
         for d in sorted({h % 8, -h % 8}):
             xb_got(1, d)
@@ -385,46 +477,42 @@
         slot = pl.ds(offs[h], m)
         got(CS.at[1, slot], cs_r.at[h])
         GO[slot] = (Q[slot] + CS[1, slot].astype(F32)).astype(BF)
-        for i, n in enumerate(blocks_of(h)):
-            at = offs[h] + i
-
-            @pl.when(n == me_d)
+        for at, dev, slot, own in gin_targets(h):
+            @pl.when(own)
             def _():
-                GI[chip_d, core] = GO[at]
-
-            @pl.when(n != me_d)
+                GI[slot, y, core] = GO[at]
+
+            @pl.when(jnp.logical_not(own))
             def _():
-                dev = (lax.div(n, 8), lax.rem(n, 8), col)
-                rc(GO.at[at], GI.at[chip_d, core], gi_s.at[at], gi_r.at[me_d], dev).start()
-
-    back_part(4)
+                rc(GO.at[at], GI.at[slot, y, core], gi_s.at[at], gi_r.at[slot, y, core], dev).start()
+
+    back_part(4, 3)
     rs_start_x(4)
     rs_start_z(0)
     rs_start_z(1)
-    back_part(3)
+    ag_step(0, 1, (1,))
     rs_start_x(3)
-    back_part(2)
+    back_part(2, 1, 0)
     rs_start_x(2)
-    back_part(1)
-    rs_start_x(1)
-    back_part(0)
-    rs_start_x(0)
     rs_step(0, 0, 1)
     rs_start_z(2)
+    rs_start_x(1)
+    rs_start_x(0)
+    xb_send(0, 1)
     feature_dp(1)
     rs_step(1, 0, 1)
     rs_step(0, 2)
     feature_pass(1)
     rs_step(2, 0, 1)
     rs_step(1, 2)
-    ag_step(0, 2, (0,))
     rs_last_far()
     rs_step(2, 2)
-    ag_step(0, 2, (2, 1))
+    ag_step(0, 2, (2,), pass_x=False)
     rs_last_near()
     ag_start(1, 0)
     rs_last_x()
     ag_start(1, 2)
+    ag_step(0, 2, (2,), take=False, pass_z=False)
     wcopy_in.wait()
     feature_end(1)
     feature_drain(0)
@@ -432,69 +520,60 @@
     rs_drain()
     ag_pair(1)
     ag_step(1, 1)
-    ag_step(0, 3, pass_z=False)
+    ag_step(0, 3, (2,))
     gin_part(0)
     for d in (0, 1, 7, 2, 6):
         xb_got(0, d)
+    for di, sg in enumerate(SIGN):
+        for lane in (0, 1):
+            z_got(0, di, 2, lane, -sg * 2)
     out_part((0, 1, 2), 0, 6)
     ag_step(1, 2)
     gin_send(0)
     gin_part(1)
     in_part((0, 1), 0, 6)
     ag_step(1, 3)
-    ag_step(0, 3, take=False, pass_x=False)
+    ag_step(0, 2, (0, 1), take=False)
     gin_send(1)
     gin_part(2)
+    ag_last(1, (2,))
+    ag_last(0, (2,))
     in_part((2,), 0, 6)
-    ag_last(1)
+    ag_last(1, (0, 1))
     gin_send(2)
     gin_part(3)
     gin_part(4)
-    ag_last(0)
     gin_send(3)
+    ag_step(0, 3, (0, 1))
     in_part((3, 4), 0, 3)
     gin_send(4)
     in_part((3, 4), 3, 6)
+    gin_relay()
     for d in (3, 5, 4):
         xb_got(0, d)
-    out_part((3, 4), 0, 6)
+    out_part((3, 4), 3, 6)
+    ag_last(0, (0, 1))
+    out_part((3, 4), 0, 3)
     ag_drain(0)
 
-    def gi_wait(j, _):
-        t = lax.rem(me_d + j, 16)
-        got(GI.at[lax.div(t, 2), lax.rem(t, 2)], gi_r.at[t])
-        return 0
-
-    lax.fori_loop(1, 16, gi_wait, 0)
-
-    def gin_sum(i, _):
-        rows = pl.ds(pl.multiple_of(i * 16, 16), 16)
-        for c in range(2):
-            total = GI[0, c, rows].astype(F32)
-            for j in range(1, 8):
-                total = total + GI[j, c, rows].astype(F32)
-            gin_o[rows, c * HD:(c + 1) * HD] = total.astype(BF)
-        return 0
-
-    lax.fori_loop(0, 5, gin_sum, 0)
+    gin_final()
 
     ag_drain(1)
-    for k in range(2):
-        @pl.when(jnp.logical_not(jnp.logical_and(dp == k, dp == xh)))
-        def _():
-            rc(pre.at[k], PRE.at[0], p_s.at[k], p_r.at[0], sib).wait_send()
+    for c, cols in enumerate(groups):
+        for k in range(2):
+            @pl.when(jnp.logical_not(jnp.logical_and(dp == k, dp == xh)))
+            def _():
+                rc(PK.at[k, :, cols], PRE.at[0, :, cols], p_s.at[c, k], p_r.at[c, 0], sib).wait_send()
     for h in range(5):
         slot = pl.ds(offs[h], offs[h + 1] - offs[h])
         rc(CS.at[0, slot], CS.at[1, slot], cs_s.at[h], cs_r.at[h], sib).wait_send()
-        for i, n in enumerate(blocks_of(h)):
-            @pl.when(n != me_d)
+        for at, _, _, own in gin_targets(h):
+            @pl.when(jnp.logical_not(own))
             def _():
-                at = offs[h] + i
-                rc(GO.at[at], GI.at[0, 0], gi_s.at[at], gi_r.at[0], sib).wait_send()
+                rc(GO.at[at], GI.at[0, 0, 0], gi_s.at[at], gi_r.at[0, 0, 0], sib).wait_send()
 
 
 def body(inputs, upstream, preact, w_in, w_out):
-    pre = jnp.swapaxes(preact, 0, 1)
     vmem = pl.BlockSpec(memory_space=pltpu.VMEM)
     hbm = pl.BlockSpec(memory_space=pl.ANY)
     dma = pltpu.SemaphoreType.DMA
@@ -505,7 +584,7 @@
             pltpu.VMEM((D, H), BF),
             pltpu.VMEM((H, D), BF),
         ),
-        in_specs=[vmem, vmem, vmem, hbm, hbm],
+        in_specs=[hbm, hbm, hbm, hbm, hbm],
         out_specs=(vmem, vmem, vmem),
         scratch_shapes=[
             pltpu.VMEM((2, 16, B, D), BF),
@@ -514,6 +593,8 @@
             pltpu.VMEM((H, D), F32),
             pltpu.VMEM((D, H), BF),
             pltpu.VMEM((H, D), BF),
+            pltpu.VMEM((40, 2, H), BF),
+            pltpu.VMEM((2, 40, H), BF),
             pltpu.VMEM((2, 40, H), BF),
             pltpu.VMEM((B, H), F32),
             pltpu.VMEM((2, 4, 2, B, HA), BF),
@@ -526,13 +607,14 @@
             pltpu.VMEM((2, 16, B, HD), BF),
             pltpu.VMEM((16, B, HD), F32),
             pltpu.VMEM((16, B, HD), BF),
-            pltpu.VMEM((8, 2, B, HD), BF),
-            dma((2,)), dma((2,)), dma((2,)),
+            pltpu.VMEM((2, 4, 2, B, HD), BF),
+            pltpu.VMEM((2, B, D), BF),
+            dma((5,)), dma((2, 2)), dma((2, 2)),
             dma((2, 16)), dma((2, 8)), dma((2, 8)),
             dma((2, 2, 4, 3)), dma((2, 2, 4, 3)),
             dma((2,)), dma((2,)), dma((2, 8)), dma((2, 8)),
             dma((2, 4, 3)), dma((2, 4, 3)), dma((8,)), dma((8,)), dma((2,)),
-            dma((5,)), dma((5,)), dma((16,)), dma((16,)),
+            dma((5,)), dma((5,)), dma((2, 4, 2)), dma((16,)), dma((1,)), dma((1,)),
         ],
         compiler_params=pltpu.CompilerParams(
             collective_id=0, has_side_effects=True, vmem_limit_bytes=56 * 2**20
@@ -540,7 +622,7 @@
         cost_estimate=pl.CostEstimate(
             flops=4 * 2 * 1280 * D * H, bytes_accessed=5 * 2 * D * H, transcendentals=B * H
         ),
-    )(inputs, upstream, pre, w_in.reshape(D, H), w_out.reshape(H, D))
+    )(inputs, upstream, preact, w_in.reshape(D, H), w_out.reshape(H, D))
     return grad_in, grad_w_in.reshape(w_in.shape), grad_w_out.reshape(w_out.shape)
 
 

time: 128 us -> 117 us (0.914)
  Pallas kernels: 122 us -> 112 us
  local copies, waits for them, and re-layouts: 5.13 us -> 3.46 us
    pallas_call x1, Pallas kernels: 122 us -> 112 us  [body(): pl.pallas_call(kernel, out_shape=(jax.ShapeDtypeStruct((B, D), BF), pltpu...]
    unnamed x6 -> x5, local copies, waits for them, and re-layouts: 5.13 us -> 3.46 us
where the time goes in v3:
time: 117 us
  Pallas kernels  112 us (96%)
  local copies, waits for them, and re-layouts  3.46 us (3%)
    pallas_call x1, Pallas kernels, body(): pl.pallas_call(kernel, out_shape=(jax.ShapeDtypeStruct((B, D), BF), pltpu...  112 us
    unnamed x5, local copies, waits for them, and re-layouts  3.46 us

profile of v3, /device:TPU:16, one launch (start us, length us, event | category | flops | bytes accessed | tf_op | source)
XLA Modules:
  0.0 116.5 jit_solution(251835628850081804)
XLA Ops:
  0.6 112.4 %shard_map.76 = (bf16[80,768]{1,0:T(8,128)(2,1)}, bf16[768,1536]{1,0:T(8,128)(2,1)S(1)}, bf16[1536,768]{1,0:T(8,128)(2,1)S(1)}) custom-call(bf16[80,768]{1,0:T(8,128)(2,1)} %inp.1, bf16[80,768]{1,0:T(8,128)(2,1)} %ups.1, bf16[40,2,1536]{2,1,0:T(2,128)(2,1)} %pre.1, bf16[768,1536]{1,0:T(8,128)(2,1)} %bitcast.6, bf16[1536,768]{1,0:T(8,128)(2,1)} %bitcast.7), custom_call_target="tpu_custom_call" | custom-call | flops 12079595520 | bytes 11796480 | tf_op jit(solution)/shard_map/pallas_call | solution.py:580
  113.0 1.4 %copy.11 = bf16[768,1,1536]{2,0,1:T(8,128)(2,1)} copy(bf16[768,1,1536]{2,0,1:T(8,128)(2,1)S(1)} %bitcast.5) | data formatting | bytes 4718592
  114.5 0.0 copy-start
  114.5 1.4 %copy.12 = bf16[1,1536,768]{2,1,0:T(8,128)(2,1)} copy(bf16[1,1536,768]{2,1,0:T(8,128)(2,1)S(1)} %bitcast.4) | data formatting | bytes 4718592
  115.9 0.0 copy-done
  115.9 0.6 copy.13
Async XLA Ops:
  114.5 1.4 %copy-start = (bf16[80,768]{1,0:T(8,128)(2,1)S(1)}, bf16[80,768]{1,0:T(8,128)(2,1)}, u32[]{:S(2)}) copy-start(bf16[80,768]{1,0:T(8,128)(2,1)} %get-tuple-element.15) | copy-start | bytes 368644

commit v4 on v3

--- a/solution.py
+++ b/solution.py
@@ -108,7 +108,8 @@
         copy.wait()
     both = PV[...]
     for k in range(2):
-        PK[k] = both[:, k, :]
+        PK[k] = jnp.zeros((48, H), BF)
+        PK[k, :40] = both[:, k, :]
     pl.semaphore_wait(barrier, 19)
 
     dpp = (1 - dp, row, col)
@@ -175,7 +176,7 @@
         cols = groups[c]
         for i in range(2):
             got(PRE.at[i, :, cols], p_r.at[c, i])
-        wide = jnp.concatenate([PRE[0, :, cols].astype(F32), PRE[1, :, cols].astype(F32)], axis=0)
+        wide = jnp.concatenate([PRE[0, :, cols].astype(F32)[:40], PRE[1, :, cols].astype(F32)[:40]], axis=0)
         active, slope = gelu_parts(wide)
         AG[0, n_me, :, cols] = active.astype(BF)
         SL[:, cols] = slope
@@ -531,24 +532,25 @@
     ag_step(1, 2)
     gin_send(0)
     gin_part(1)
+    ag_step(1, 3, (2,))
     in_part((0, 1), 0, 6)
-    ag_step(1, 3)
+    ag_step(1, 3, (0, 1))
     ag_step(0, 2, (0, 1), take=False)
     gin_send(1)
     gin_part(2)
     ag_last(1, (2,))
     ag_last(0, (2,))
-    in_part((2,), 0, 6)
     ag_last(1, (0, 1))
     gin_send(2)
     gin_part(3)
+    in_part((2, 3, 4), 0, 2)
+    gin_send(3)
     gin_part(4)
-    gin_send(3)
     ag_step(0, 3, (0, 1))
-    in_part((3, 4), 0, 3)
+    in_part((2, 3, 4), 2, 3)
     gin_send(4)
-    in_part((3, 4), 3, 6)
     gin_relay()
+    in_part((2, 3, 4), 3, 6)
     for d in (3, 5, 4):
         xb_got(0, d)
     out_part((3, 4), 3, 6)
@@ -573,6 +575,16 @@
                 rc(GO.at[at], GI.at[0, 0, 0], gi_s.at[at], gi_r.at[0, 0, 0], sib).wait_send()
 
 
+def write_out(a, b, c, a_o, b_o, c_o, sems):
+    copies = [
+        pltpu.make_async_copy(src, dst, sems.at[i]) for i, (src, dst) in enumerate(((b, b_o), (c, c_o), (a, a_o)))
+    ]
+    for copy in copies:
+        copy.start()
+    for copy in copies:
+        copy.wait()
+
+
 def body(inputs, upstream, preact, w_in, w_out):
     vmem = pl.BlockSpec(memory_space=pltpu.VMEM)
     hbm = pl.BlockSpec(memory_space=pl.ANY)
@@ -580,7 +592,7 @@
     grad_in, grad_w_in, grad_w_out = pl.pallas_call(
         kernel,
         out_shape=(
-            jax.ShapeDtypeStruct((B, D), BF),
+            pltpu.VMEM((B, D), BF),
             pltpu.VMEM((D, H), BF),
             pltpu.VMEM((H, D), BF),
         ),
@@ -594,8 +606,8 @@
             pltpu.VMEM((D, H), BF),
             pltpu.VMEM((H, D), BF),
             pltpu.VMEM((40, 2, H), BF),
-            pltpu.VMEM((2, 40, H), BF),
-            pltpu.VMEM((2, 40, H), BF),
+            pltpu.VMEM((2, 48, H), BF),
+            pltpu.VMEM((2, 48, H), BF),
             pltpu.VMEM((B, H), F32),
             pltpu.VMEM((2, 4, 2, B, HA), BF),
             pltpu.VMEM((2, 4, 2, B, HA), BF),
@@ -623,6 +635,15 @@
             flops=4 * 2 * 1280 * D * H, bytes_accessed=5 * 2 * D * H, transcendentals=B * H
         ),
     )(inputs, upstream, preact, w_in.reshape(D, H), w_out.reshape(H, D))
+    results = (grad_in, grad_w_in, grad_w_out)
+    grad_in, grad_w_in, grad_w_out = pl.pallas_call(
+        write_out,
+        out_shape=tuple(jax.ShapeDtypeStruct(x.shape, x.dtype) for x in results),
+        in_specs=[hbm] * 3,
+        out_specs=(hbm,) * 3,
+        scratch_shapes=[dma((3,))],
+        compiler_params=pltpu.CompilerParams(vmem_limit_bytes=2**20),
+    )(*(pltpu.with_memory_space_constraint(x, pltpu.VMEM) for x in results))
     return grad_in, grad_w_in.reshape(w_in.shape), grad_w_out.reshape(w_out.shape)
 
 

time: 117 us -> 115 us (0.983)
  local copies, waits for them, and re-layouts: 3.46 us -> 0 us
  Pallas kernels: 112 us -> 114 us
    unnamed x5 -> x0, local copies, waits for them, and re-layouts: 3.46 us -> none
    pallas_call x1 -> x2, Pallas kernels: 112 us -> 114 us  [the longest x1 112 us: body(): pl.pallas_call(kernel, out_shape=(pltpu.VMEM((B, D), BF), pltpu.VMEM((D,...]
where the time goes in v4:
time: 115 us
  Pallas kernels  114 us (99%)
    pallas_call x1, Pallas kernels, body(): pl.pallas_call(kernel, out_shape=(pltpu.VMEM((B, D), BF), pltpu.VMEM((D,...  112 us

profile of v4, /device:TPU:16, one launch (start us, length us, event | category | flops | bytes accessed | tf_op | source)
XLA Modules:
  0.0 114.8 jit_solution(2574298892280612772)
XLA Ops:
  0.6 111.9 %shard_map.76 = (bf16[80,768]{1,0:T(8,128)(2,1)S(1)}, bf16[768,1536]{1,0:T(8,128)(2,1)S(1)}, bf16[1536,768]{1,0:T(8,128)(2,1)S(1)}) custom-call(bf16[80,768]{1,0:T(8,128)(2,1)} %inp.1, bf16[80,768]{1,0:T(8,128)(2,1)} %ups.1, bf16[40,2,1536]{2,1,0:T(2,128)(2,1)} %pre.1, bf16[768,1536]{1,0:T(8,128)(2,1)} %bitcast.4, bf16[1536,768]{1,0:T(8,128)(2,1)} %bitcast.5), custom_call_target="tpu_custom_call" | custom-call | flops 12079595520 | bytes 11796480 | tf_op jit(solution)/shard_map/pallas_call | solution.py:592
  112.5 2.2 %shard_map.77 = (bf16[80,768]{1,0:T(8,128)(2,1)}, bf16[768,1536]{1,0:T(8,128)(2,1)}, bf16[1536,768]{1,0:T(8,128)(2,1)}) custom-call(bf16[80,768]{1,0:T(8,128)(2,1)S(1)} %get-tuple-element.9.a, bf16[768,1536]{1,0:T(8,128)(2,1)S(1)} %get-tuple-element.10.b, bf16[1536,768]{1,0:T(8,128)(2,1)S(1)} %get-tuple-element.11.c), custom_call_target="tpu_custom_call" | custom-call | tf_op jit(solution)/shard_map/pallas_call | solution.py:639

commit v5 on v4

--- a/solution.py
+++ b/solution.py
@@ -537,8 +537,8 @@
     ag_step(1, 3, (0, 1))
     ag_step(0, 2, (0, 1), take=False)
     gin_send(1)
+    ag_last(1, (2,))
     gin_part(2)
-    ag_last(1, (2,))
     ag_last(0, (2,))
     ag_last(1, (0, 1))
     gin_send(2)

time: 115 us -> 116 us (level)
  no operation moved by 1% of the time
where the time goes in v5:
time: 116 us; the launch traced here: 115 us
  Pallas kernels  114 us (98%)
    pallas_call x1, Pallas kernels, body(): pl.pallas_call(kernel, out_shape=(pltpu.VMEM((B, D), BF), pltpu.VMEM((D,...  112 us

profile of v5, /device:TPU:16, one launch (start us, length us, event | category | flops | bytes accessed | tf_op | source)
XLA Modules:
  0.0 114.7 jit_solution(3984039321515293203)
XLA Ops:
  0.6 111.9 %shard_map.76 = (bf16[80,768]{1,0:T(8,128)(2,1)S(1)}, bf16[768,1536]{1,0:T(8,128)(2,1)S(1)}, bf16[1536,768]{1,0:T(8,128)(2,1)S(1)}) custom-call(bf16[80,768]{1,0:T(8,128)(2,1)} %inp.1, bf16[80,768]{1,0:T(8,128)(2,1)} %ups.1, bf16[40,2,1536]{2,1,0:T(2,128)(2,1)} %pre.1, bf16[768,1536]{1,0:T(8,128)(2,1)} %bitcast.4, bf16[1536,768]{1,0:T(8,128)(2,1)} %bitcast.5), custom_call_target="tpu_custom_call" | custom-call | flops 12079595520 | bytes 11796480 | tf_op jit(solution)/shard_map/pallas_call | solution.py:592
  112.5 2.2 %shard_map.77 = (bf16[80,768]{1,0:T(8,128)(2,1)}, bf16[768,1536]{1,0:T(8,128)(2,1)}, bf16[1536,768]{1,0:T(8,128)(2,1)}) custom-call(bf16[80,768]{1,0:T(8,128)(2,1)S(1)} %get-tuple-element.9.a, bf16[768,1536]{1,0:T(8,128)(2,1)S(1)} %get-tuple-element.10.b, bf16[1536,768]{1,0:T(8,128)(2,1)S(1)} %get-tuple-element.11.c), custom_call_target="tpu_custom_call" | custom-call | tf_op jit(solution)/shard_map/pallas_call | solution.py:639
